TPU v7x, 32 devices: a whole 2x2x4 slice. The times are simulated.
32 devices in a mesh: ep: 8 (over y, x, core), gd: 4 (over z).
Axes of the slice: x: 2, y: 2, z: 4, core: 2. Of those that a mesh axis runs over, the one named last changes fastest.
Arguments:
- tokens: bfloat16 [256, 4096], P(('ep', 'gd')), may hold values from -6 to 6
- expert_ids: int32 [256, 4], P(('ep', 'gd')), may hold values from 0 to 7, all different within a row; in each aligned block of 8 rows (0 to 7, 8 to 15, ...) at most 6 rows name the same one
- combine: float32 [256, 4], P(('ep', 'gd')), may hold values from 0.02 to 0.3
- w_gate: bfloat16 [8, 4096, 1536], P('ep', None, 'gd'), may hold values from -0.09375 to 0.09375
- w_up: bfloat16 [8, 4096, 1536], P('ep', None, 'gd'), may hold values from -0.09375 to 0.09375
- w_down: bfloat16 [8, 1536, 4096], P('ep', 'gd'), may hold values from -0.15625 to 0.15625
- w_query: bfloat16 [4096, 2048], P(None, 'gd'), may hold values from -0.09375 to 0.09375
- w_key: bfloat16 [4096, 512], P(None, 'gd'), may hold values from -0.09375 to 0.09375
- w_value: bfloat16 [4096, 512], P(None, 'gd'), may hold values from -0.09375 to 0.09375
- cache_keys: bfloat16 [256, 4, 64, 128], P('ep', 'gd'), may hold values from -68 to 68
- cache_values: bfloat16 [256, 4, 64, 128], P('ep', 'gd'), may hold values from -6 to 6
- lengths: int32 [256], P('ep'), may hold values from 1 to 64, as said below
Outputs:
- stream: bfloat16 [256, 4096], P(('ep', 'gd'))
- guard: bfloat16 [256, 2048], P('ep', 'gd')
Inputs may be any that keep to these rules, and one draw needn't show every extreme that they name: `expert_ids`: each row names 4 different experts; in the rows of one device no expert is named by more than 6 rows. `lengths`: some row has the full window of 64 positions.
All inputs are finite; a program needn't handle non-finite values.
Results may differ from a plain program's by a relative error of at most 0.03.
Values may be sent and summed in bfloat16 or wider, within the bound.
A program may use at most 128 MiB of HBM per device.

v0:
```python
import math

import jax
import jax.numpy as jnp
from jax import lax
from jax.sharding import PartitionSpec as P

EPSILON = 1e-06


def norm_rows(values):
    widened = values.astype(jnp.float32)
    return (
        widened * lax.rsqrt(jnp.mean(widened * widened, axis=-1, keepdims=True) + EPSILON)
    ).astype(jnp.bfloat16)


def slot_numbers(chosen, experts):
    blocks_n, rows_n, picks_n = chosen.shape
    flat_ids = chosen.reshape(blocks_n, rows_n * picks_n)
    onehot = (flat_ids[:, :, None] == jnp.arange(experts, dtype=jnp.int32)[None, None, :]).astype(
        jnp.int32
    )
    before = jnp.cumsum(onehot, axis=1) - onehot
    return jnp.sum(before * onehot, axis=-1).reshape(blocks_n, rows_n, picks_n)


def build_slots(row_blocks, targets, slots_n):
    wanted = jnp.any(
        targets[:, None, :, :] == jnp.arange(slots_n, dtype=jnp.int32)[None, :, None, None], axis=-1
    )
    selector = wanted.astype(jnp.bfloat16)
    return jnp.einsum(
        "bsr,brd->bsd", selector, row_blocks, preferred_element_type=jnp.float32
    ).astype(jnp.bfloat16)


def per_device(
    tokens,
    expert_ids,
    combine,
    w_gate,
    w_up,
    w_down,
    w_query,
    w_key,
    w_value,
    cache_keys,
    cache_values,
    lengths,
):
    rows_n, width = tokens.shape
    picks_n = expert_ids.shape[1]
    experts = lax.axis_size("ep")
    members = lax.axis_size("gd")
    capacity = max(2, 3 * rows_n * picks_n // (2 * experts))
    slots_n = experts * capacity
    normed = norm_rows(tokens)
    own_slot = slot_numbers(expert_ids[None], experts)[0]
    own_dest = expert_ids * capacity + own_slot
    group_normed, group_ids = (
        lax.all_gather(normed, "gd", axis=0, tiled=True),
        lax.all_gather(expert_ids, "gd", axis=0, tiled=True),
    )
    group_ids = group_ids.reshape(members, rows_n, picks_n)
    group_dest = group_ids * capacity + slot_numbers(group_ids, experts)
    outgoing = build_slots(group_normed.reshape(members, rows_n, width), group_dest, slots_n)
    outgoing = outgoing.reshape(members, experts, capacity, width)
    arrived = lax.all_to_all(outgoing, "ep", split_axis=1, concat_axis=1, tiled=True)
    slot_rows = arrived.reshape(-1, width)
    gate_val = jnp.dot(slot_rows, w_gate[0], preferred_element_type=jnp.float32)
    up_val = jnp.dot(slot_rows, w_up[0], preferred_element_type=jnp.float32)
    active = (jax.nn.silu(gate_val) * up_val).astype(jnp.bfloat16)
    partial_out = jnp.dot(active, w_down[0], preferred_element_type=jnp.float32).astype(
        jnp.bfloat16
    )
    summed = lax.psum_scatter(
        lax.optimization_barrier(partial_out).astype(jnp.float32).astype(jnp.bfloat16),
        "gd",
        scatter_dimension=0,
        tiled=True,
    ).astype(jnp.float32)
    returned = lax.all_to_all(
        summed.reshape(experts, capacity, width), "ep", split_axis=0, concat_axis=0, tiled=True
    )
    matches = own_dest[:, :, None] == jnp.arange(slots_n, dtype=jnp.int32)[None, None, :]
    weight_rows = jnp.sum(jnp.where(matches, combine[:, :, None], 0.0), axis=1)
    mixture = jnp.dot(
        weight_rows,
        returned.reshape(slots_n, width),
        precision=lax.Precision.HIGHEST,
        preferred_element_type=jnp.float32,
    )
    stream = (tokens.astype(jnp.float32) + mixture).astype(jnp.bfloat16)
    group_stream = lax.all_gather(stream, "gd", axis=0, tiled=True)
    guard_norm = norm_rows(group_stream)
    queries = jnp.dot(guard_norm, w_query, preferred_element_type=jnp.float32)
    key_new = jnp.dot(guard_norm, w_key, preferred_element_type=jnp.float32).astype(jnp.bfloat16)
    value_new = jnp.dot(guard_norm, w_value, preferred_element_type=jnp.float32).astype(
        jnp.bfloat16
    )
    group_total, heads_kv, window_len, head_size = cache_keys.shape
    heads_per = w_query.shape[1] // (heads_kv * head_size)
    queries = queries.reshape(group_total, heads_kv, heads_per, head_size)
    key_new = key_new.reshape(group_total, heads_kv, head_size)
    value_new = value_new.reshape(group_total, heads_kv, head_size)
    scale_factor = 1.0 / math.sqrt(head_size)
    scores = (
        jnp.einsum(
            "rhgd,rhjd->rhgj",
            queries,
            cache_keys.astype(jnp.float32),
            precision=lax.Precision.HIGHEST,
        )
        * scale_factor
    )
    own_score = (
        jnp.einsum(
            "rhgd,rhd->rhg", queries, key_new.astype(jnp.float32), precision=lax.Precision.HIGHEST
        )
        * scale_factor
    )
    positions = jnp.arange(window_len, dtype=jnp.int32)
    allowed = positions[None, None, None, :] >= (window_len - lengths)[:, None, None, None]
    masked = jnp.where(allowed, scores, -jnp.inf)
    highest = jnp.maximum(jnp.max(masked, axis=-1), own_score)
    weights = jnp.exp(masked - highest[..., None])
    own_weight = jnp.exp(own_score - highest)
    denominator = jnp.sum(weights, axis=-1) + own_weight
    probabilities = weights / denominator[..., None]
    own_prob = own_weight / denominator
    attended = jnp.einsum(
        "rhgj,rhjd->rhgd",
        probabilities,
        cache_values.astype(jnp.float32),
        precision=lax.Precision.HIGHEST,
    )
    attended = attended + own_prob[..., None] * value_new.astype(jnp.float32)[:, :, None, :]
    guard = attended.astype(jnp.bfloat16).reshape(group_total, heads_kv * heads_per * head_size)
    return (stream, guard)


def solution(mesh):
    return jax.shard_map(
        per_device,
        mesh=mesh,
        in_specs=(
            P(("ep", "gd"), None),
            P(("ep", "gd"), None),
            P(("ep", "gd"), None),
            P("ep", None, "gd"),
            P("ep", None, "gd"),
            P("ep", "gd", None),
            P(None, "gd"),
            P(None, "gd"),
            P(None, "gd"),
            P("ep", "gd", None, None),
            P("ep", "gd", None, None),
            P("ep"),
        ),
        out_specs=(P(("ep", "gd"), None), P("ep", "gd")),
        check_vma=False,
    )
```

profile of v0, /device:TPU:0, one launch (start us, length us, event | category | flops | bytes accessed | tf_op | source)
XLA Modules:
  0.0 170.2 jit_solution(11120883383770120948)
XLA Ops:
  7.2 0.0 copy-start
  7.2 0.0 reduce-scatter.2.cloned.1.call-start
  7.2 13.8 %all-gather = s32[4,8,4]{1,2,0:T(4,128)S(1)} all-gather(s32[1,8,4]{1,2,0:T(4,128)} %bitcast.51), channel_id=1, replica_groups=mesh['ep'=8,'gd'=4] {'gd'}, dimensions={0}, use_global_device_ids=true | all-gather | bytes 640 | tf_op jit(solution)/shard_map/all_gather | solution.py:63
  21.0 0.1 copy.38
  21.1 0.1 eq.75
  21.2 0.1 fusion.32
  21.3 0.1 reduce_window_sum.23
  21.4 0.2 select_reduce_fusion
  21.6 0.1 reshape.236
  21.7 0.1 copy.40
  21.8 0.1 fusion.33
  21.9 1.0 fusion.29
  22.9 0.9 fusion.30
  23.8 14.0 %all_gather.10 = bf16[32,4096]{1,0:T(8,128)(2,1)S(1)} all-gather(bf16[8,4096]{1,0:T(8,128)(2,1)S(1)} %fusion.30), channel_id=1, replica_groups=mesh['ep'=8,'gd'=4] {'gd'}, dimensions={0}, use_global_device_ids=true | all-gather | bytes 327680 | tf_op jit(solution)/shard_map/all_gather | solution.py:62
  37.8 0.6 convolution_convert_fusion.1
  38.5 1.2 copy.41
  39.7 24.5 %all_to_all.10 = bf16[4,8,6,4096]{3,0,2,1:T(4,128)(2,1)S(1)} all-to-all(bf16[4,8,6,4096]{3,0,2,1:T(4,128)(2,1)S(1)} %bitcast.46), channel_id=1, replica_groups=mesh['ep'=8,'gd'=4] {'ep'}, dimensions={1} | all-to-all | bytes 3145728 | tf_op jit(solution)/shard_map/all_to_all | solution.py:69
  64.2 2.2 %copy.42 = bf16[4,8,6,4096]{3,2,1,0:T(8,128)(2,1)} copy(bf16[4,8,6,4096]{3,0,2,1:T(4,128)(2,1)S(1)} %all_to_all.10) | data formatting | bytes 3145728 | tf_op jit(solution)/shard_map/all_to_all | solution.py:69
  66.4 3.7 %reshape.239 = bf16[192,4096]{1,0:T(8,128)(2,1)} reshape(bf16[4,8,6,4096]{3,2,1,0:T(8,128)(2,1)} %copy.42) | data formatting | bytes 3145728 | tf_op jit(solution)/shard_map/reshape | solution.py:70
  70.1 3.3 %fusion.4 = f32[192,384]{1,0:T(8,128)S(1)} fusion(bf16[192,4096]{1,0:T(8,128)(2,1)} %reshape.239, bf16[1,4096,384]{2,1,0:T(8,128)(2,1)} %param.15), kind=kOutput, calls=%fused_computation.7 | convolution fusion | flops 603979776 | bytes 5013504 | tf_op jit(solution)/shard_map/dot_general | solution.py:71
  73.4 5.4 %convolution_convert_fusion = bf16[192,4096]{1,0:T(8,128)(2,1)} fusion(bf16[1,384,4096]{2,1,0:T(8,128)(2,1)S(1)} %copy-done, bf16[192,4096]{1,0:T(8,128)(2,1)} %reshape.239, bf16[1,4096,384]{2,1,0:T(8,128)(2,1)} %param.16, f32[192,384]{1,0:T(8,128)S(1)} %fusion.4), kind=kOutput, calls=%fused_computation | convolution fusion | flops 1209188352 | bytes 9732096 | tf_op jit(solution)/shard_map/dot_general | solution.py:74
  78.9 0.0 reduce-scatter.2.cloned.1.call-update
  78.9 0.1 copy.35
  79.0 0.1 eq.68
  79.1 0.1 fusion.37
  79.2 0.1 reduce_window_sum.22
  79.2 0.2 select_reduce_fusion.2
  79.4 0.1 squeeze_reshape.3
  79.5 32.7 %reduce-scatter.2.cloned.1.call-done = bf16[48,4096]{1,0:T(8,128)(2,1)} async-done(((bf16[192,4096]{1,0:T(8,128)(2,1)}), bf16[48,4096]{1,0:T(8,128)(2,1)}) %reduce-scatter.2.cloned.1.call-update) | async-done | bytes 393232 | tf_op jit(solution)/shard_map/reduce_scatter | solution.py:77
  112.2 2.1 %reshape.248 = f32[8,6,4096]{2,1,0:T(8,128)} reshape(bf16[48,4096]{1,0:T(8,128)(2,1)} %reduce-scatter.2.cloned.1.call-done) | data formatting | bytes 1179648 | tf_op jit(solution)/shard_map/reshape | solution.py:84
  114.3 4.2 %all-to-all-start.1 = ((f32[8,6,4096]{2,1,0:T(8,128)}), f32[8,6,4096]{2,1,0:T(8,128)}, u32[]{:S(2)}, u32[]{:S(2)}) async-start(f32[8,6,4096]{2,1,0:T(8,128)} %reshape.248), calls=%async_computation.2 | async-start | bytes 2097152 | tf_op jit(solution)/shard_map/all_to_all | solution.py:83
  118.6 0.1 copy.37
  118.7 0.1 select_reduce_fusion.1
  118.8 0.1 iota_compare_fusion.2
  118.8 15.1 %all-to-all-done.1 = f32[8,6,4096]{2,1,0:T(8,128)} async-done(((f32[8,6,4096]{2,1,0:T(8,128)}), f32[8,6,4096]{2,1,0:T(8,128)}, u32[]{:S(2)}, u32[]{:S(2)}) %all-to-all-start.1) | async-done | bytes 786464 | tf_op jit(solution)/shard_map/all_to_all | solution.py:83
  134.0 2.3 %reshape.242 = f32[48,4096]{1,0:T(8,128)} reshape(f32[8,6,4096]{2,1,0:T(8,128)} %all-to-all-done.1) | data formatting | bytes 1572864 | tf_op jit(solution)/shard_map/reshape | solution.py:90
  136.2 1.6 fusion
  137.9 13.8 %all_gather.11 = bf16[32,4096]{1,0:T(8,128)(2,1)S(1)} all-gather(bf16[8,4096]{1,0:T(8,128)(2,1)S(1)} %fusion), channel_id=1, replica_groups=mesh['ep'=8,'gd'=4] {'gd'}, dimensions={0}, use_global_device_ids=true | all-gather | bytes 327680 | tf_op jit(solution)/shard_map/all_gather | solution.py:95
  151.7 0.2 fusion.18
  151.8 3.1 %fusion.45 = f32[32,512]{1,0:T(8,128)S(1)} fusion(bf16[4096,512]{1,0:T(8,128)(2,1)} %param.18, bf16[32,4096]{1,0:T(8,128)(2,1)S(1)} %all_gather.11, f32[32]{0:T(128)S(1)} %add_rsqrt_fusion), kind=kOutput, calls=%fused_computation.65 | convolution fusion | flops 134610944 | bytes 4522112 | tf_op jit(solution)/shard_map/dot_general | solution.py:97
  154.9 0.7 reshape.243
  155.5 1.6 fusion.15
  157.2 1.1 fusion.38
  158.3 2.1 %fusion.47 = (f32[32,4]{1,0:T(8,128)S(1)}, f32[32,4,64]{2,1,0:T(4,128)S(1)}) fusion(f32[32,4,128]{2,1,0:T(4,128)} %reshape.243, bf16[32,1,64,128]{3,2,1,0:T(8,128)(2,1)} %param.21, pred[32,64]{1,0:T(8,128)(4,1)S(1)} %iota_compare_fusion.2), kind=kOutput, calls=%fused_computation.66 | convolution fusion | flops 12607360 | bytes 625152 | tf_op jit(solution)/shard_map/rhgd,rhjd->rhgj/dot_general | solution.py:109
  160.4 0.2 fusion.34
  160.6 1.6 fusion.14
  162.2 0.6 fusion.13
  162.7 0.6 copy.49
  (20 shorter events, 0.1 us)
Async XLA Ops:
  7.2 66.3 %copy-start = (bf16[1,384,4096]{2,1,0:T(8,128)(2,1)S(1)}, bf16[1,384,4096]{2,1,0:T(8,128)(2,1)}, u32[]{:S(2)}) copy-start(bf16[1,384,4096]{2,1,0:T(8,128)(2,1)} %param.17) | copy-start | bytes 9437188
  7.2 105.0 %reduce-scatter.2.cloned.1.call-start = ((), (), s32[]{:S(2)}) async-start(), calls=%async_computation.3 | async-start | bytes 1966080 | tf_op jit(solution)/shard_map/reduce_scatter | solution.py:77
  73.4 5.5 %copy-start.3 = (s32[8,4]{0,1:T(4,128)S(1)}, s32[8,4]{0,1:T(4,128)}, u32[]{:S(2)}) copy-start(s32[8,4]{0,1:T(4,128)} %param.13) | copy-start | bytes 388
  78.9 39.8 %copy-start.4 = (f32[8,4]{0,1:T(4,128)S(1)}, f32[8,4]{0,1:T(4,128)}, u32[]{:S(2)}) copy-start(f32[8,4]{0,1:T(4,128)} %param.14) | copy-start | bytes 388
  78.9 39.9 %copy-start.6 = (s32[32]{0:T(128)S(1)}, s32[32]{0:T(128)}, u32[]{:S(2)}) copy-start(s32[32]{0:T(128)} %param.23) | copy-start | bytes 388
  78.9 57.4 %copy-start.1 = (bf16[8,4096]{1,0:T(8,128)(2,1)S(1)}, bf16[8,4096]{1,0:T(8,128)(2,1)}, u32[]{:S(2)}) copy-start(bf16[8,4096]{1,0:T(8,128)(2,1)} %param.12) | copy-start | bytes 196612
  114.3 19.7 %all-to-all-start.1 = ((f32[8,6,4096]{2,1,0:T(8,128)}), f32[8,6,4096]{2,1,0:T(8,128)}, u32[]{:S(2)}, u32[]{:S(2)}) async-start(f32[8,6,4096]{2,1,0:T(8,128)} %reshape.248), calls=%async_computation.2 | async-start | bytes 2097152 | tf_op jit(solution)/shard_map/all_to_all | solution.py:83
  137.9 19.3 %copy-start.2 = (bf16[8,4096]{1,0:T(8,128)(2,1)}, bf16[8,4096]{1,0:T(8,128)(2,1)S(1)}, u32[]{:S(2)}) copy-start(bf16[8,4096]{1,0:T(8,128)(2,1)S(1)} %fusion) | copy-start | bytes 196612
  155.5 6.6 %copy-start.5 = (bf16[32,1,64,128]{3,2,1,0:T(8,128)(2,1)S(1)}, bf16[32,1,64,128]{3,2,1,0:T(8,128)(2,1)}, u32[]{:S(2)}) copy-start(bf16[32,1,64,128]{3,2,1,0:T(8,128)(2,1)} %param.22) | copy-start | bytes 1572868
Sparse Core Ops, SparseCore 0:
  79.0 33.1 reduce-scatter.1
where the time goes:
time: 171 us; the launch traced here: 170 us
  blocking collectives  66.1 us (39%)
  waiting for transfers between devices  47.9 us (28%)
  matrix products  21 us (12%)
  between operations  14.2 us (8%)
  local copies, waits for them, and re-layouts  13.5 us (8%)
  starting transfers between devices  4.27 us (2%)
  other arithmetic  3.27 us (2%)
    reduce_scatter x1, waiting for transfers between devices, per_device(): lax.psum_scatter(lax.optimization_barrier(partial_out).astype(jnp.float32...  32.7 us
    all_to_all x1, blocking collectives, per_device(): lax.all_to_all(outgoing, 'ep', split_axis=1, concat_axis=1, tiled=True)  24.5 us
    all_to_all x1, waiting for transfers between devices, per_device(): lax.all_to_all(summed.reshape(experts, capacity, width), 'ep', split_axis...  15.1 us
    all_gather x1, blocking collectives, per_device(): lax.all_gather(normed, 'gd', axis=0, tiled=True)  14 us
    all_gather x1, blocking collectives, per_device(): lax.all_gather(expert_ids, 'gd', axis=0, tiled=True)  13.8 us
    all_gather x1, blocking collectives, per_device(): group_stream = lax.all_gather(stream, 'gd', axis=0, tiled=True)  13.8 us
    dot_general x1, matrix products, per_device(): jnp.dot(active, w_down[0], preferred_element_type=jnp.float32)  5.43 us
    all_to_all x1, starting transfers between devices, per_device(): lax.all_to_all(summed.reshape(experts, capacity, width), 'ep', split_axis...  4.23 us
  transfers between devices with their start and end apart: 2, of which 2 were waited for; matrix products, arithmetic and copies ran while one was open for 0% of the time, Pallas kernels for 0%

commit v1 on v0

--- a/solution.py
+++ b/solution.py
@@ -1,8 +1,11 @@
+import functools
 import math
 
 import jax
 import jax.numpy as jnp
 from jax import lax
+from jax.experimental import pallas as pl
+from jax.experimental.pallas import tpu as pltpu
 from jax.sharding import PartitionSpec as P
 
 EPSILON = 1e-06
@@ -140,9 +143,454 @@
     return (stream, guard)
 
 
+CORES = 2
+CHIPS = 4
+CHUNKS = 4
+MESH = pl.DeviceIdType.MESH
+
+
+def fused_kernel(
+    groups,
+    tokens_ref,
+    ids_ref,
+    combine_ref,
+    lengths_ref,
+    gate_hbm,
+    up_hbm,
+    down_hbm,
+    query_hbm,
+    key_hbm,
+    value_hbm,
+    cache_k_hbm,
+    cache_v_hbm,
+    stream_ref,
+    guard_ref,
+    w_in,
+    w_out,
+    w_guard,
+    keys,
+    values,
+    rows_in,
+    rows_all,
+    weight_all,
+    hidden,
+    active,
+    part,
+    got_core,
+    sum_core,
+    got_chip,
+    sum_chip,
+    got_z,
+    stream_all,
+    load_sem,
+    z_send,
+    z_recv,
+    x_send,
+    x_recv,
+    y_send,
+    y_recv,
+    d_send,
+    d_recv,
+    c_send,
+    c_recv,
+    r1_send,
+    r1_recv,
+    r2_send,
+    r2_recv,
+    r3_send,
+    r3_recv,
+    s_send,
+    s_recv,
+):
+    rows_n, width = tokens_ref.shape
+    half = width // 2
+    unit = gate_hbm.shape[2]
+    me_e = lax.axis_index("ep")
+    g = lax.axis_index("gd")
+    core = me_e % CORES
+    chip = me_e // CORES
+    x, y = chip % 2, chip // 2
+    x_chip = y * 2 + (1 - x)
+    y_chip = (1 - y) * 2 + x
+    d_chip = (1 - y) * 2 + (1 - x)
+    sibling = (chip * CORES + (1 - core), g)
+    x_dev = (x_chip * CORES + core, g)
+    y_dev = (y_chip * CORES + core, g)
+    d_dev = (d_chip * CORES + core, g)
+
+    def z_of(step):
+        return (g + step) % groups
+
+    loads = []
+
+    def load(src, dst):
+        copy = pltpu.make_async_copy(src, dst, load_sem.at[len(loads)])
+        copy.start()
+        loads.append(copy)
+
+    barrier = pltpu.get_barrier_semaphore()
+    peers = [sibling, x_dev, y_dev, d_dev] + [(me_e, z_of(k)) for k in range(1, groups)]
+    for peer in peers:
+        pl.semaphore_signal(barrier, inc=1, device_id=peer, device_id_type=MESH)
+
+    load(gate_hbm.at[0], w_in.at[:, 0:unit])
+    load(up_hbm.at[0], w_in.at[:, unit : 2 * unit])
+    load(down_hbm.at[0], w_out)
+    q_n, k_n = query_hbm.shape[1], key_hbm.shape[1]
+    load(query_hbm, w_guard.at[:, 0:q_n])
+    load(key_hbm, w_guard.at[:, q_n : q_n + k_n])
+    load(value_hbm, w_guard.at[:, q_n + k_n : q_n + 2 * k_n])
+    load(cache_k_hbm, keys)
+    load(cache_v_hbm, values)
+
+    wide = tokens_ref[...].astype(jnp.float32)
+    normed = wide * lax.rsqrt(jnp.mean(wide * wide, axis=-1, keepdims=True) + EPSILON)
+    lanes = lax.broadcasted_iota(jnp.int32, (rows_n, 128), 1)
+    table = jnp.zeros((rows_n, 128), jnp.float32)
+    for k in range(ids_ref.shape[1]):
+        table = table + jnp.where(lanes == ids_ref[:, k : k + 1], combine_ref[:, k : k + 1], 0.0)
+    table_top = table.astype(jnp.bfloat16).astype(jnp.float32)
+    packed = jnp.concatenate([normed[:, :half], normed[:, half:]], axis=0)
+    rows_in[core, chip, g, :, 0:half] = packed.astype(jnp.bfloat16)
+    rows_in[core, chip, g, :, half : half + 128] = jnp.concatenate(
+        [table_top, table - table_top], axis=0
+    ).astype(jnp.bfloat16)
+
+    pl.semaphore_wait(barrier, len(peers))
+
+    sends = []
+
+    def send(src, dst, send_sem, recv_sem, device):
+        copy = pltpu.make_async_remote_copy(
+            src_ref=src,
+            dst_ref=dst,
+            send_sem=send_sem,
+            recv_sem=recv_sem,
+            device_id=device,
+            device_id_type=MESH,
+        )
+        copy.start()
+        sends.append(copy)
+        return copy
+
+    def row_send(chip_of, step, send_sem, recv_sem, device):
+        block = rows_in.at[core, chip_of, (g + groups - step) % groups]
+        return send(block, block, send_sem, recv_sem, device)
+
+    z_copies, x_copies, y_copies, d_copies, c_copies = {}, {}, {}, {}, {}
+
+    def share(kind, chip_of, step):
+        c_copies[kind, step] = row_send(
+            chip_of, step, c_send.at[kind, step], c_recv.at[kind, step], sibling
+        )
+
+    def spread(step):
+        x_copies[step] = row_send(chip, step, x_send.at[step], x_recv.at[step], x_dev)
+        y_copies[step] = row_send(chip, step, y_send.at[step], y_recv.at[step], y_dev)
+        share(0, chip, step)
+
+    def forward(step):
+        x_copies[step].wait_recv()
+        if step % 2 == 1:
+            d_copies[step] = row_send(x_chip, step, d_send.at[step], d_recv.at[step], y_dev)
+        share(1, x_chip, step)
+        y_copies[step].wait_recv()
+        if step % 2 == 0:
+            d_copies[step] = row_send(y_chip, step, d_send.at[step], d_recv.at[step], x_dev)
+        share(2, y_chip, step)
+
+    for k in range(1, groups):
+        z_copies[k] = row_send(chip, 0, z_send.at[k], z_recv.at[k], (me_e, z_of(k)))
+    spread(0)
+    for k in range(1, groups):
+        z_copies[k].wait_recv()
+        spread(k)
+        forward(k - 1)
+    forward(groups - 1)
+    for k in range(groups):
+        d_copies[k].wait_recv()
+        share(3, d_chip, k)
+    for k in range(groups):
+        for kind in range(4):
+            c_copies[kind, k].wait_recv()
+
+    group_rows = groups * rows_n
+
+    def unpack(block, carry):
+        c, h = block // CHIPS, block % CHIPS
+        start = pl.multiple_of(block * group_rows, group_rows)
+        for side in range(2):
+            got = rows_in[c, h, :, :, 0:half].astype(jnp.float32)
+            got = got[:, side * rows_n : (side + 1) * rows_n].reshape(group_rows, half)
+            rows_all[pl.ds(start, group_rows), side * half : (side + 1) * half] = got.astype(
+                jnp.bfloat16
+            )
+        extra = rows_in[c, h, :, :, half : half + 128].astype(jnp.float32)
+        weight_all[pl.ds(start, group_rows), :] = (extra[:, :rows_n] + extra[:, rows_n:]).reshape(
+            group_rows, 128
+        )
+        return carry
+
+    lax.fori_loop(0, CORES * CHIPS, unpack, 0)
+
+    loads[0].wait()
+    loads[1].wait()
+    tile = 256
+
+    def first(n, carry):
+        cols = pl.ds(pl.multiple_of(n * tile, tile), tile)
+        hidden[:, cols] = jnp.dot(
+            rows_all[...], w_in[:, cols], preferred_element_type=jnp.float32
+        )
+        return carry
+
+    lax.fori_loop(0, 2 * unit // tile, first, 0)
+    table_all = weight_all[...]
+    picked = lax.broadcasted_iota(jnp.int32, table_all.shape, 1) == me_e
+    row_weight = jnp.sum(jnp.where(picked, table_all, 0.0), axis=-1, keepdims=True)
+    gate_val = hidden[:, 0:unit]
+    active[...] = (
+        gate_val / (1.0 + jnp.exp(-gate_val)) * hidden[:, unit : 2 * unit] * row_weight
+    ).astype(jnp.bfloat16)
+    loads[2].wait()
+
+    span = width // CHUNKS
+    piece = span // 2
+    r1, r2, r3, s_copies = {}, {}, {}, {}
+
+    def expert_chunk(t):
+        blocks_n = CORES * CHIPS * groups
+        for side in range(2):
+            lower = t * span + side * piece
+            out = jnp.dot(
+                active[...], w_out[:, lower : lower + piece], preferred_element_type=jnp.float32
+            ).reshape(CORES, CHIPS, groups, rows_n, piece)
+            if side == 0:
+                top = out
+        part[t] = jnp.concatenate([top, out], axis=3).astype(jnp.bfloat16)
+        r1[t] = send(
+            part.at[t, 1 - core], got_core.at[t], r1_send.at[t], r1_recv.at[t], sibling
+        )
+
+    def chip_chunk(t):
+        r1[t].wait_recv()
+        total = part[t, core].astype(jnp.float32) + got_core[t].astype(jnp.float32)
+        sum_core[t] = total.astype(jnp.bfloat16)
+        for kind, (chip_to, device) in enumerate(
+            ((d_chip, d_dev), (x_chip, x_dev), (y_chip, y_dev))
+        ):
+            r2[t, kind] = send(
+                sum_core.at[t, chip_to],
+                got_chip.at[t, kind],
+                r2_send.at[t, kind],
+                r2_recv.at[t, kind],
+                device,
+            )
+
+    def z_chunk(t):
+        total = sum_core[t, chip].astype(jnp.float32)
+        for kind in range(3):
+            r2[t, kind].wait_recv()
+            total = total + got_chip[t, kind].astype(jnp.float32)
+        sum_chip[t] = total.astype(jnp.bfloat16)
+        for k in range(1, groups):
+            r3[t, k] = send(
+                sum_chip.at[t, z_of(k)],
+                got_z.at[t, k],
+                r3_send.at[t, k],
+                r3_recv.at[t, k],
+                (me_e, z_of(k)),
+            )
+
+    def stream_chunk(t):
+        total = sum_chip[t, g].astype(jnp.float32)
+        for k in range(1, groups):
+            r3[t, k].wait_recv()
+            total = total + got_z[t, k].astype(jnp.float32)
+        mixture = jnp.concatenate([total[:rows_n], total[rows_n:]], axis=1)
+        cols = slice(t * span, (t + 1) * span)
+        stream = tokens_ref[:, cols].astype(jnp.float32) + mixture
+        stream_ref[:, cols] = stream.astype(jnp.bfloat16)
+        stream_all[t, g] = jnp.concatenate(
+            [stream[:, :piece], stream[:, piece:]], axis=0
+        ).astype(jnp.bfloat16)
+        for k in range(1, groups):
+            block = stream_all.at[t, g]
+            s_copies[t, k] = send(
+                block, block, s_send.at[t, k], s_recv.at[t, k], (me_e, z_of(k))
+            )
+
+    state = {}
+
+    def guard_chunk(t):
+        for k in range(1, groups):
+            s_copies[t, k].wait_recv()
+        got = stream_all[t].astype(jnp.float32)
+        if t == 0:
+            for i in range(3, 8):
+                loads[i].wait()
+        for side in range(2):
+            rows = got[:, side * rows_n : (side + 1) * rows_n].reshape(group_rows, piece)
+            lower = t * span + side * piece
+            product = jnp.dot(
+                rows.astype(jnp.bfloat16),
+                w_guard[lower : lower + piece, :],
+                preferred_element_type=jnp.float32,
+            )
+            square = jnp.sum(rows * rows, axis=-1, keepdims=True)
+            if t == 0 and side == 0:
+                state["qkv"], state["square"] = product, square
+            else:
+                state["qkv"] = state["qkv"] + product
+                state["square"] = state["square"] + square
+
+    stages = (expert_chunk, chip_chunk, z_chunk, stream_chunk, guard_chunk)
+    for step in range(CHUNKS + len(stages) - 1):
+        for late, stage in enumerate(stages):
+            if 0 <= step - late < CHUNKS:
+                stage(step - late)
+
+    qkv = state["qkv"] * lax.rsqrt(state["square"] / width + EPSILON)
+    head = keys.shape[1]
+    heads = q_n // head
+    window = keys.shape[0] // group_rows
+    scale = 1.0 / math.sqrt(head)
+    query = jnp.concatenate([qkv[:, h * head : (h + 1) * head] for h in range(heads)], axis=0)
+    key_new = qkv[:, q_n : q_n + k_n].astype(jnp.bfloat16).astype(jnp.float32)
+    value_new = qkv[:, q_n + k_n :].astype(jnp.bfloat16).astype(jnp.float32)
+    key_new = jnp.concatenate([key_new] * heads, axis=0)
+    value_new = jnp.concatenate([value_new] * heads, axis=0)
+    allowed_n = jnp.concatenate([lengths_ref[...]] * heads, axis=0)
+    all_rows = heads * group_rows
+    own_score = jnp.sum(query * key_new, axis=-1, keepdims=True) * scale
+    scores = None
+    rest = query
+    for _ in range(3):
+        top = rest.astype(jnp.bfloat16)
+        rest = rest - top.astype(jnp.float32)
+        term = lax.dot_general(
+            top, keys[...], (((1,), (1,)), ((), ())), preferred_element_type=jnp.float32
+        )
+        scores = term if scores is None else scores + term
+    scores = scores * scale
+    column = lax.broadcasted_iota(jnp.int32, scores.shape, 1)
+    row = lax.broadcasted_iota(jnp.int32, (all_rows, 1), 0) % group_rows
+    upper = (row + 1) * window
+    allowed = (column >= upper - allowed_n) & (column < upper)
+    masked = jnp.where(allowed, scores, -jnp.inf)
+    highest = jnp.maximum(jnp.max(masked, axis=-1, keepdims=True), own_score)
+    weights = jnp.exp(masked - highest)
+    own_weight = jnp.exp(own_score - highest)
+    denominator = jnp.sum(weights, axis=-1, keepdims=True) + own_weight
+    attended = own_weight * value_new
+    rest = weights
+    for _ in range(2):
+        top = rest.astype(jnp.bfloat16)
+        rest = rest - top.astype(jnp.float32)
+        attended = attended + jnp.dot(top, values[...], preferred_element_type=jnp.float32)
+    attended = attended / denominator
+    guard_ref[...] = jnp.concatenate(
+        [attended[h * group_rows : (h + 1) * group_rows] for h in range(heads)], axis=1
+    ).astype(jnp.bfloat16)
+    for copy in sends:
+        copy.wait_send()
+
+
+def fused_device(
+    tokens,
+    expert_ids,
+    combine,
+    w_gate,
+    w_up,
+    w_down,
+    w_query,
+    w_key,
+    w_value,
+    cache_keys,
+    cache_values,
+    lengths,
+):
+    rows_n, width = tokens.shape
+    groups = lax.axis_size("gd")
+    unit = w_gate.shape[2]
+    group_rows, heads_kv, window, head = cache_keys.shape
+    total_rows = CORES * CHIPS * groups * rows_n
+    piece = width // CHUNKS // 2
+    pack = 2 * rows_n
+    guard_n = w_query.shape[1] + w_key.shape[1] + w_value.shape[1]
+    bf16, f32 = jnp.bfloat16, jnp.float32
+    dma = pltpu.SemaphoreType.DMA
+    in_vmem = pl.BlockSpec(memory_space=pltpu.VMEM)
+    in_any = pl.BlockSpec(memory_space=pl.ANY)
+    return pl.pallas_call(
+        functools.partial(fused_kernel, groups),
+        out_shape=(
+            jax.ShapeDtypeStruct((rows_n, width), bf16),
+            jax.ShapeDtypeStruct((group_rows, w_query.shape[1]), bf16),
+        ),
+        in_specs=[in_vmem] * 4 + [in_any] * 8,
+        out_specs=(in_vmem, in_vmem),
+        scratch_shapes=[
+            pltpu.VMEM((width, 2 * unit), bf16),
+            pltpu.VMEM((unit, width), bf16),
+            pltpu.VMEM((width, guard_n), bf16),
+            pltpu.VMEM((group_rows * window, head), bf16),
+            pltpu.VMEM((group_rows * window, head), bf16),
+            pltpu.VMEM((CORES, CHIPS, groups, pack, width // 2 + 128), bf16),
+            pltpu.VMEM((total_rows, width), bf16),
+            pltpu.VMEM((total_rows, 128), f32),
+            pltpu.VMEM((total_rows, 2 * unit), f32),
+            pltpu.VMEM((total_rows, unit), bf16),
+            pltpu.VMEM((CHUNKS, CORES, CHIPS, groups, pack, piece), bf16),
+            pltpu.VMEM((CHUNKS, CHIPS, groups, pack, piece), bf16),
+            pltpu.VMEM((CHUNKS, CHIPS, groups, pack, piece), bf16),
+            pltpu.VMEM((CHUNKS, 3, groups, pack, piece), bf16),
+            pltpu.VMEM((CHUNKS, groups, pack, piece), bf16),
+            pltpu.VMEM((CHUNKS, groups, pack, piece), bf16),
+            pltpu.VMEM((CHUNKS, groups, pack, piece), bf16),
+            dma((8,)),
+            dma((groups,)),
+            dma((groups,)),
+            dma((groups,)),
+            dma((groups,)),
+            dma((groups,)),
+            dma((groups,)),
+            dma((groups,)),
+            dma((groups,)),
+            dma((4, groups)),
+            dma((4, groups)),
+            dma((CHUNKS,)),
+            dma((CHUNKS,)),
+            dma((CHUNKS, 3)),
+            dma((CHUNKS, 3)),
+            dma((CHUNKS, groups)),
+            dma((CHUNKS, groups)),
+            dma((CHUNKS, groups)),
+            dma((CHUNKS, groups)),
+        ],
+        compiler_params=pltpu.CompilerParams(
+            collective_id=0, has_side_effects=True, vmem_limit_bytes=52 * 1024 * 1024
+        ),
+    )(
+        tokens,
+        expert_ids,
+        combine,
+        lengths.reshape(group_rows, 1),
+        w_gate,
+        w_up,
+        w_down,
+        w_query,
+        w_key,
+        w_value,
+        cache_keys.reshape(group_rows * heads_kv * window, head),
+        cache_values.reshape(group_rows * heads_kv * window, head),
+    )
+
+
 def solution(mesh):
+    fused = mesh.shape["ep"] == 8 and mesh.shape["gd"] == 4
     return jax.shard_map(
-        per_device,
+        fused_device if fused else per_device,
         mesh=mesh,
         in_specs=(
             P(("ep", "gd"), None),

time: 171 us -> 59.4 us (0.35)
  blocking collectives: 66.1 us -> 0 us
  Pallas kernels: 0 us -> 52 us
  waiting for transfers between devices: 47.9 us -> 0 us
  matrix products: 21 us -> 0 us
  between operations: 14.2 us -> 0.64 us
  local copies, waits for them, and re-layouts: 13.5 us -> 6.41 us
  starting transfers between devices: 4.27 us -> 0 us
  other arithmetic: 3.27 us -> 0 us
    pallas_call x0 -> x1, Pallas kernels: none -> 52 us  [fused_device(): pl.pallas_call(functools.partial(fused_kernel, groups), out_shape=(jax.Sh...]
    all_gather x3 -> x0, blocking collectives: 41.6 us -> none  [the longest x1 14 us: per_device(): lax.all_gather(normed, 'gd', axis=0, tiled=True)]
    reduce_scatter x1 -> x0, waiting for transfers between devices: 32.7 us -> none  [per_device(): lax.psum_scatter(lax.optimization_barrier(partial_out).astype(jnp.float32...]
    all_to_all x1 -> x0, blocking collectives: 24.5 us -> none  [per_device(): lax.all_to_all(outgoing, 'ep', split_axis=1, concat_axis=1, tiled=True)]
    dot_general x10 -> x0, matrix products: 21 us -> none  [the longest x1 5.43 us: per_device(): jnp.dot(active, w_down[0], preferred_element_type=jnp.float32)]
    all_to_all x1 -> x0, waiting for transfers between devices: 15.1 us -> none  [per_device(): lax.all_to_all(summed.reshape(experts, capacity, width), 'ep', split_axis...]
    reshape x4 -> x1, local copies, waits for them, and re-layouts: 8.13 us -> 0.74 us  [fused_device(): lengths.reshape(group_rows, 1)]
    unnamed x16 -> x10, local copies, waits for them, and re-layouts: 0.75 us -> 5.68 us
  transfers between devices with their start and end apart: 2 -> 0, of which waited for: 2 -> 0; matrix products, arithmetic and copies ran while one was open for 0% -> 0% of each run, Pallas kernels for 0% -> 0%
where the time goes in v1:
time: 59.4 us; the launch traced here: 59.1 us
  Pallas kernels  52 us (88%)
  local copies, waits for them, and re-layouts  6.41 us (11%)
  between operations  0.64 us (1%)
    pallas_call x1, Pallas kernels, fused_device(): pl.pallas_call(functools.partial(fused_kernel, groups), out_shape=(jax.Sh...  52 us
    unnamed x10, local copies, waits for them, and re-layouts  5.68 us

profile of v1, /device:TPU:0, one launch (start us, length us, event | category | flops | bytes accessed | tf_op | source)
XLA Modules:
  0.0 59.1 jit_solution(7487642335113102195)
XLA Ops:
  0.6 0.8 %copy.14.ids_ref = s32[8,4]{1,0:T(8,128)S(1)} copy(s32[8,4]{0,1:T(4,128)} %param.13) | data formatting | bytes 256 | tf_op args[1]
  1.4 0.8 %copy.15.combine_ref = f32[8,4]{1,0:T(8,128)S(1)} copy(f32[8,4]{0,1:T(4,128)} %param.14) | data formatting | bytes 256 | tf_op args[2]
  2.1 0.7 %copy.16.lengths_ref = s32[32,1]{1,0:T(8,128)S(1)} copy(s32[32,1]{0,1:T(1,128)} %bitcast.5) | data formatting | bytes 256 | tf_op jit(solution)/shard_map/reshape | solution.py:578
  2.9 0.0 copy-start
  2.9 1.0 %copy-done = bf16[32,1,64,128]{3,2,1,0:T(8,128)(2,1)S(1)} copy-done((bf16[32,1,64,128]{3,2,1,0:T(8,128)(2,1)S(1)}, bf16[32,1,64,128]{3,2,1,0:T(8,128)(2,1)}, u32[]{:S(2)}) %copy-start) | copy-done | bytes 524312
  3.9 0.0 copy-start.1
  3.9 1.0 %copy-done.1 = bf16[32,1,64,128]{3,2,1,0:T(8,128)(2,1)S(1)} copy-done((bf16[32,1,64,128]{3,2,1,0:T(8,128)(2,1)S(1)}, bf16[32,1,64,128]{3,2,1,0:T(8,128)(2,1)}, u32[]{:S(2)}) %copy-start.1) | copy-done | bytes 524312
  5.0 0.0 copy-start.2
  5.0 0.8 %copy-done.2 = bf16[8,4096]{1,0:T(8,128)(2,1)S(1)} copy-done((bf16[8,4096]{1,0:T(8,128)(2,1)S(1)}, bf16[8,4096]{1,0:T(8,128)(2,1)}, u32[]{:S(2)}) %copy-start.2) | copy-done | bytes 65560
  5.8 52.0 %shard_map.131 = (bf16[8,4096]{1,0:T(8,128)(2,1)S(1)}, bf16[32,512]{1,0:T(8,128)(2,1)S(1)}) custom-call(bf16[8,4096]{1,0:T(8,128)(2,1)S(1)} %copy-done.2, s32[8,4]{1,0:T(8,128)S(1)} %copy.14.ids_ref, f32[8,4]{1,0:T(8,128)S(1)} %copy.15.combine_ref, s32[32,1]{1,0:T(8,128)S(1)} %copy.16.lengths_ref, bf16[1,4096,384]{2,1,0:T(8,128)(2,1)} %gate_hbm.1, ...), custom_call_target="tpu_custom_call" | custom-call | tf_op jit(solution)/shard_map/pallas_call | solution.py:525
  57.8 0.6 %copy.19 = bf16[8,4096]{1,0:T(8,128)(2,1)} copy(bf16[8,4096]{1,0:T(8,128)(2,1)S(1)} %get-tuple-element.4) | data formatting | bytes 131072
  58.5 0.6 %copy.20 = bf16[32,512]{1,0:T(8,128)(2,1)} copy(bf16[32,512]{1,0:T(8,128)(2,1)S(1)} %get-tuple-element.5) | data formatting | bytes 65536
Async XLA Ops:
  2.9 1.0 %copy-start = (bf16[32,1,64,128]{3,2,1,0:T(8,128)(2,1)S(1)}, bf16[32,1,64,128]{3,2,1,0:T(8,128)(2,1)}, u32[]{:S(2)}) copy-start(bf16[32,1,64,128]{3,2,1,0:T(8,128)(2,1)} %param.21) | copy-start | bytes 1572868
  3.9 1.0 %copy-start.1 = (bf16[32,1,64,128]{3,2,1,0:T(8,128)(2,1)S(1)}, bf16[32,1,64,128]{3,2,1,0:T(8,128)(2,1)}, u32[]{:S(2)}) copy-start(bf16[32,1,64,128]{3,2,1,0:T(8,128)(2,1)} %param.22) | copy-start | bytes 1572868
  5.0 0.8 %copy-start.2 = (bf16[8,4096]{1,0:T(8,128)(2,1)S(1)}, bf16[8,4096]{1,0:T(8,128)(2,1)}, u32[]{:S(2)}) copy-start(bf16[8,4096]{1,0:T(8,128)(2,1)} %tokens_ref.1) | copy-start | bytes 196612

commit v2 on v1

--- a/solution.py
+++ b/solution.py
@@ -145,16 +145,23 @@
 
 CORES = 2
 CHIPS = 4
-CHUNKS = 4
+CHUNKS = 8
 MESH = pl.DeviceIdType.MESH
+
+
+def as_column(line):
+    size = line.shape[1]
+    across = lax.broadcasted_iota(jnp.int32, (size, size), 1)
+    down = lax.broadcasted_iota(jnp.int32, (size, size), 0)
+    return jnp.sum(jnp.where(across == down, line, 0.0), axis=1, keepdims=True)
 
 
 def fused_kernel(
     groups,
-    tokens_ref,
-    ids_ref,
-    combine_ref,
-    lengths_ref,
+    tokens_hbm,
+    ids_hbm,
+    combine_hbm,
+    lengths_hbm,
     gate_hbm,
     up_hbm,
     down_hbm,
@@ -165,6 +172,10 @@
     cache_v_hbm,
     stream_ref,
     guard_ref,
+    tokens_ref,
+    ids_ref,
+    combine_ref,
+    lengths_ref,
     w_in,
     w_out,
     w_guard,
@@ -179,6 +190,7 @@
     got_core,
     sum_core,
     got_chip,
+    sum_mid,
     sum_chip,
     got_z,
     stream_all,
@@ -202,7 +214,7 @@
     s_send,
     s_recv,
 ):
-    rows_n, width = tokens_ref.shape
+    rows_n, width = tokens_hbm.shape
     half = width // 2
     unit = gate_hbm.shape[2]
     me_e = lax.axis_index("ep")
@@ -216,7 +228,6 @@
     sibling = (chip * CORES + (1 - core), g)
     x_dev = (x_chip * CORES + core, g)
     y_dev = (y_chip * CORES + core, g)
-    d_dev = (d_chip * CORES + core, g)
 
     def z_of(step):
         return (g + step) % groups
@@ -229,10 +240,14 @@
         loads.append(copy)
 
     barrier = pltpu.get_barrier_semaphore()
-    peers = [sibling, x_dev, y_dev, d_dev] + [(me_e, z_of(k)) for k in range(1, groups)]
+    peers = [sibling, x_dev, y_dev] + [(me_e, z_of(k)) for k in range(1, groups)]
     for peer in peers:
         pl.semaphore_signal(barrier, inc=1, device_id=peer, device_id_type=MESH)
 
+    load(tokens_hbm, tokens_ref)
+    load(ids_hbm, ids_ref)
+    load(combine_hbm, combine_ref)
+    load(lengths_hbm, lengths_ref)
     load(gate_hbm.at[0], w_in.at[:, 0:unit])
     load(up_hbm.at[0], w_in.at[:, unit : 2 * unit])
     load(down_hbm.at[0], w_out)
@@ -243,12 +258,16 @@
     load(cache_k_hbm, keys)
     load(cache_v_hbm, values)
 
+    for i in range(3):
+        loads[i].wait()
     wide = tokens_ref[...].astype(jnp.float32)
     normed = wide * lax.rsqrt(jnp.mean(wide * wide, axis=-1, keepdims=True) + EPSILON)
     lanes = lax.broadcasted_iota(jnp.int32, (rows_n, 128), 1)
     table = jnp.zeros((rows_n, 128), jnp.float32)
-    for k in range(ids_ref.shape[1]):
-        table = table + jnp.where(lanes == ids_ref[:, k : k + 1], combine_ref[:, k : k + 1], 0.0)
+    for k in range(ids_ref.shape[0]):
+        named = as_column(ids_ref[k : k + 1, :].astype(jnp.float32)).astype(jnp.int32)
+        share_of = as_column(combine_ref[k : k + 1, :])
+        table = table + jnp.where(lanes == named, share_of, 0.0)
     table_top = table.astype(jnp.bfloat16).astype(jnp.float32)
     packed = jnp.concatenate([normed[:, :half], normed[:, half:]], axis=0)
     rows_in[core, chip, g, :, 0:half] = packed.astype(jnp.bfloat16)
@@ -333,8 +352,8 @@
 
     lax.fori_loop(0, CORES * CHIPS, unpack, 0)
 
-    loads[0].wait()
-    loads[1].wait()
+    loads[4].wait()
+    loads[5].wait()
     tile = 256
 
     def first(n, carry):
@@ -352,7 +371,7 @@
     active[...] = (
         gate_val / (1.0 + jnp.exp(-gate_val)) * hidden[:, unit : 2 * unit] * row_weight
     ).astype(jnp.bfloat16)
-    loads[2].wait()
+    loads[6].wait()
 
     span = width // CHUNKS
     piece = span // 2
@@ -376,20 +395,28 @@
         r1[t].wait_recv()
         total = part[t, core].astype(jnp.float32) + got_core[t].astype(jnp.float32)
         sum_core[t] = total.astype(jnp.bfloat16)
-        for kind, (chip_to, device) in enumerate(
-            ((d_chip, d_dev), (x_chip, x_dev), (y_chip, y_dev))
-        ):
+        first_chip, first_dev = (x_chip, x_dev) if t % 2 == 0 else (y_chip, y_dev)
+        for kind, chip_to in ((1, d_chip), (0, first_chip)):
             r2[t, kind] = send(
                 sum_core.at[t, chip_to],
                 got_chip.at[t, kind],
                 r2_send.at[t, kind],
                 r2_recv.at[t, kind],
-                device,
+                first_dev,
             )
+
+    def mid_chunk(t):
+        second_chip, second_dev = (y_chip, y_dev) if t % 2 == 0 else (x_chip, x_dev)
+        r2[t, 1].wait_recv()
+        total = sum_core[t, second_chip].astype(jnp.float32) + got_chip[t, 1].astype(jnp.float32)
+        sum_mid[t] = total.astype(jnp.bfloat16)
+        r2[t, 2] = send(
+            sum_mid.at[t], got_chip.at[t, 2], r2_send.at[t, 2], r2_recv.at[t, 2], second_dev
+        )
 
     def z_chunk(t):
         total = sum_core[t, chip].astype(jnp.float32)
-        for kind in range(3):
+        for kind in (0, 2):
             r2[t, kind].wait_recv()
             total = total + got_chip[t, kind].astype(jnp.float32)
         sum_chip[t] = total.astype(jnp.bfloat16)
@@ -427,7 +454,7 @@
             s_copies[t, k].wait_recv()
         got = stream_all[t].astype(jnp.float32)
         if t == 0:
-            for i in range(3, 8):
+            for i in (3, 7, 8, 9, 10, 11):
                 loads[i].wait()
         for side in range(2):
             rows = got[:, side * rows_n : (side + 1) * rows_n].reshape(group_rows, piece)
@@ -444,7 +471,7 @@
                 state["qkv"] = state["qkv"] + product
                 state["square"] = state["square"] + square
 
-    stages = (expert_chunk, chip_chunk, z_chunk, stream_chunk, guard_chunk)
+    stages = (expert_chunk, chip_chunk, mid_chunk, z_chunk, stream_chunk, guard_chunk)
     for step in range(CHUNKS + len(stages) - 1):
         for late, stage in enumerate(stages):
             if 0 <= step - late < CHUNKS:
@@ -455,43 +482,56 @@
     heads = q_n // head
     window = keys.shape[0] // group_rows
     scale = 1.0 / math.sqrt(head)
-    query = jnp.concatenate([qkv[:, h * head : (h + 1) * head] for h in range(heads)], axis=0)
     key_new = qkv[:, q_n : q_n + k_n].astype(jnp.bfloat16).astype(jnp.float32)
     value_new = qkv[:, q_n + k_n :].astype(jnp.bfloat16).astype(jnp.float32)
-    key_new = jnp.concatenate([key_new] * heads, axis=0)
-    value_new = jnp.concatenate([value_new] * heads, axis=0)
-    allowed_n = jnp.concatenate([lengths_ref[...]] * heads, axis=0)
-    all_rows = heads * group_rows
-    own_score = jnp.sum(query * key_new, axis=-1, keepdims=True) * scale
-    scores = None
-    rest = query
-    for _ in range(3):
-        top = rest.astype(jnp.bfloat16)
-        rest = rest - top.astype(jnp.float32)
-        term = lax.dot_general(
-            top, keys[...], (((1,), (1,)), ((), ())), preferred_element_type=jnp.float32
-        )
-        scores = term if scores is None else scores + term
-    scores = scores * scale
-    column = lax.broadcasted_iota(jnp.int32, scores.shape, 1)
-    row = lax.broadcasted_iota(jnp.int32, (all_rows, 1), 0) % group_rows
-    upper = (row + 1) * window
-    allowed = (column >= upper - allowed_n) & (column < upper)
-    masked = jnp.where(allowed, scores, -jnp.inf)
-    highest = jnp.maximum(jnp.max(masked, axis=-1, keepdims=True), own_score)
-    weights = jnp.exp(masked - highest)
-    own_weight = jnp.exp(own_score - highest)
-    denominator = jnp.sum(weights, axis=-1, keepdims=True) + own_weight
-    attended = own_weight * value_new
-    rest = weights
-    for _ in range(2):
-        top = rest.astype(jnp.bfloat16)
-        rest = rest - top.astype(jnp.float32)
-        attended = attended + jnp.dot(top, values[...], preferred_element_type=jnp.float32)
-    attended = attended / denominator
-    guard_ref[...] = jnp.concatenate(
-        [attended[h * group_rows : (h + 1) * group_rows] for h in range(heads)], axis=1
-    ).astype(jnp.bfloat16)
+    lengths_n = as_column(lengths_ref[...].astype(jnp.float32)).astype(jnp.int32)
+    span_keys = rows_n * window
+    outs = []
+    for a in range(groups):
+        here = slice(a * rows_n, (a + 1) * rows_n)
+        query = jnp.concatenate([qkv[here, h * head : (h + 1) * head] for h in range(heads)], axis=0)
+        key_own = jnp.concatenate([key_new[here]] * heads, axis=0)
+        value_own = jnp.concatenate([value_new[here]] * heads, axis=0)
+        allowed_n = jnp.concatenate([lengths_n[here]] * heads, axis=0)
+        own_score = jnp.sum(query * key_own, axis=-1, keepdims=True) * scale
+        pieces, rest = [], query
+        for _ in range(3):
+            top = rest.astype(jnp.bfloat16).astype(jnp.float32)
+            pieces.append(top)
+            rest = rest - top
+        product = lax.dot_general(
+            jnp.concatenate(pieces, axis=0).astype(jnp.bfloat16),
+            keys[a * span_keys : (a + 1) * span_keys, :],
+            (((1,), (1,)), ((), ())),
+            preferred_element_type=jnp.float32,
+        )
+        all_rows = heads * rows_n
+        scores = (
+            product[:all_rows] + product[all_rows : 2 * all_rows] + product[2 * all_rows :]
+        ) * scale
+        column = lax.broadcasted_iota(jnp.int32, scores.shape, 1)
+        row = lax.broadcasted_iota(jnp.int32, (all_rows, 1), 0) % rows_n
+        upper = (row + 1) * window
+        allowed = (column >= upper - allowed_n) & (column < upper)
+        masked = jnp.where(allowed, scores, -jnp.inf)
+        highest = jnp.maximum(jnp.max(masked, axis=-1, keepdims=True), own_score)
+        weights = jnp.exp(masked - highest)
+        own_weight = jnp.exp(own_score - highest)
+        denominator = jnp.sum(weights, axis=-1, keepdims=True) + own_weight
+        top = weights.astype(jnp.bfloat16).astype(jnp.float32)
+        product = jnp.dot(
+            jnp.concatenate([top, weights - top], axis=0).astype(jnp.bfloat16),
+            values[a * span_keys : (a + 1) * span_keys, :],
+            preferred_element_type=jnp.float32,
+        )
+        attended = product[:all_rows] + product[all_rows:] + own_weight * value_own
+        attended = attended / denominator
+        outs.append(
+            jnp.concatenate(
+                [attended[h * rows_n : (h + 1) * rows_n] for h in range(heads)], axis=1
+            )
+        )
+    guard_ref[...] = jnp.concatenate(outs, axis=0).astype(jnp.bfloat16)
     for copy in sends:
         copy.wait_send()
 
@@ -528,9 +568,13 @@
             jax.ShapeDtypeStruct((rows_n, width), bf16),
             jax.ShapeDtypeStruct((group_rows, w_query.shape[1]), bf16),
         ),
-        in_specs=[in_vmem] * 4 + [in_any] * 8,
+        in_specs=[in_any] * 12,
         out_specs=(in_vmem, in_vmem),
         scratch_shapes=[
+            pltpu.VMEM((rows_n, width), bf16),
+            pltpu.VMEM((expert_ids.shape[1], rows_n), jnp.int32),
+            pltpu.VMEM((combine.shape[1], rows_n), f32),
+            pltpu.VMEM((1, group_rows), jnp.int32),
             pltpu.VMEM((width, 2 * unit), bf16),
             pltpu.VMEM((unit, width), bf16),
             pltpu.VMEM((width, guard_n), bf16),
@@ -548,7 +592,8 @@
             pltpu.VMEM((CHUNKS, groups, pack, piece), bf16),
             pltpu.VMEM((CHUNKS, groups, pack, piece), bf16),
             pltpu.VMEM((CHUNKS, groups, pack, piece), bf16),
-            dma((8,)),
+            pltpu.VMEM((CHUNKS, groups, pack, piece), bf16),
+            dma((12,)),
             dma((groups,)),
             dma((groups,)),
             dma((groups,)),
@@ -569,13 +614,13 @@
             dma((CHUNKS, groups)),
         ],
         compiler_params=pltpu.CompilerParams(
-            collective_id=0, has_side_effects=True, vmem_limit_bytes=52 * 1024 * 1024
+            collective_id=0, has_side_effects=True, vmem_limit_bytes=63 * 1024 * 1024
         ),
     )(
         tokens,
-        expert_ids,
-        combine,
-        lengths.reshape(group_rows, 1),
+        expert_ids.T,
+        combine.T,
+        lengths.reshape(1, group_rows),
         w_gate,
         w_up,
         w_down,

time: 59.4 us -> 66.3 us (1.12)
  Pallas kernels: 52 us -> 62.6 us
  local copies, waits for them, and re-layouts: 6.41 us -> 2.85 us
    pallas_call x1, Pallas kernels: 52 us -> 62.6 us  [fused_device(): pl.pallas_call(functools.partial(fused_kernel, groups), out_shape=(jax.Sh...]
    unnamed x10 -> x2, local copies, waits for them, and re-layouts: 5.68 us -> 2.85 us
    reshape x1 -> x0, local copies, waits for them, and re-layouts: 0.74 us -> none  [fused_device(): lengths.reshape(group_rows, 1)]
where the time goes in v2:
time: 66.3 us; the launch traced here: 66.1 us
  Pallas kernels  62.6 us (94%)
  local copies, waits for them, and re-layouts  2.85 us (4%)
    pallas_call x1, Pallas kernels, fused_device(): pl.pallas_call(functools.partial(fused_kernel, groups), out_shape=(jax.Sh...  62.6 us
    unnamed x2, local copies, waits for them, and re-layouts  2.85 us

profile of v2, /device:TPU:0, one launch (start us, length us, event | category | flops | bytes accessed | tf_op | source)
XLA Modules:
  0.0 66.1 jit_solution(9413326599404117847)
XLA Ops:
  0.6 62.6 %shard_map.131 = (bf16[8,4096]{1,0:T(8,128)(2,1)}, bf16[32,512]{1,0:T(8,128)(2,1)}) custom-call(bf16[8,4096]{1,0:T(8,128)(2,1)} %tokens_hbm.1, s32[4,8]{1,0:T(4,128)} %bitcast.7, f32[4,8]{1,0:T(4,128)} %bitcast.8, s32[1,32]{1,0:T(1,128)} %bitcast.9, bf16[1,4096,384]{2,1,0:T(8,128)(2,1)} %gate_hbm.1, bf16[1,4096,384]{2,1,0:T(8,128)(2,1)} %up_hbm.1, ...), custom_call_target="tpu_custom_call" | custom-call | tf_op jit(solution)/shard_map/pallas_call | solution.py:565
  63.2 1.5 %copy.16 = bf16[8,4096]{1,0:T(8,128)(2,1)} copy(bf16[8,4096]{1,0:T(8,128)(2,1)} %get-tuple-element.4) | data formatting | bytes 131072
  64.7 1.4 %copy.17 = bf16[32,512]{1,0:T(8,128)(2,1)} copy(bf16[32,512]{1,0:T(8,128)(2,1)} %get-tuple-element.5) | data formatting | bytes 65536

commit v3 on v2

--- a/solution.py
+++ b/solution.py
@@ -145,7 +145,7 @@
 
 CORES = 2
 CHIPS = 4
-CHUNKS = 8
+CHUNKS = 4
 MESH = pl.DeviceIdType.MESH
 
 
@@ -561,14 +561,14 @@
     bf16, f32 = jnp.bfloat16, jnp.float32
     dma = pltpu.SemaphoreType.DMA
     in_vmem = pl.BlockSpec(memory_space=pltpu.VMEM)
-    in_any = pl.BlockSpec(memory_space=pl.ANY)
+    in_hbm = pl.BlockSpec(memory_space=pltpu.HBM)
     return pl.pallas_call(
         functools.partial(fused_kernel, groups),
         out_shape=(
             jax.ShapeDtypeStruct((rows_n, width), bf16),
             jax.ShapeDtypeStruct((group_rows, w_query.shape[1]), bf16),
         ),
-        in_specs=[in_any] * 12,
+        in_specs=[in_hbm] * 12,
         out_specs=(in_vmem, in_vmem),
         scratch_shapes=[
             pltpu.VMEM((rows_n, width), bf16),
@@ -614,7 +614,7 @@
             dma((CHUNKS, groups)),
         ],
         compiler_params=pltpu.CompilerParams(
-            collective_id=0, has_side_effects=True, vmem_limit_bytes=63 * 1024 * 1024
+            collective_id=0, has_side_effects=True, vmem_limit_bytes=64000 * 1024
         ),
     )(
         tokens,

time: 66.3 us -> 56.2 us (0.85)
  Pallas kernels: 62.6 us -> 52.4 us
    pallas_call x1, Pallas kernels: 62.6 us -> 52.4 us  [fused_device(): pl.pallas_call(functools.partial(fused_kernel, groups), out_shape=(jax.Sh...]
where the time goes in v3:
time: 56.2 us; the launch traced here: 55.9 us
  Pallas kernels  52.4 us (93%)
  local copies, waits for them, and re-layouts  2.85 us (5%)
  between operations  0.64 us (1%)
    pallas_call x1, Pallas kernels, fused_device(): pl.pallas_call(functools.partial(fused_kernel, groups), out_shape=(jax.Sh...  52.4 us
    unnamed x2, local copies, waits for them, and re-layouts  2.85 us

profile of v3, /device:TPU:0, one launch (start us, length us, event | category | flops | bytes accessed | tf_op | source)
XLA Modules:
  0.0 55.9 jit_solution(15678138862781984816)
XLA Ops:
  0.6 52.4 %shard_map.131 = (bf16[8,4096]{1,0:T(8,128)(2,1)}, bf16[32,512]{1,0:T(8,128)(2,1)}) custom-call(bf16[8,4096]{1,0:T(8,128)(2,1)} %tokens_hbm.1, s32[4,8]{1,0:T(4,128)} %bitcast.7, f32[4,8]{1,0:T(4,128)} %bitcast.8, s32[1,32]{1,0:T(1,128)} %bitcast.9, bf16[1,4096,384]{2,1,0:T(8,128)(2,1)} %gate_hbm.1, bf16[1,4096,384]{2,1,0:T(8,128)(2,1)} %up_hbm.1, ...), custom_call_target="tpu_custom_call" | custom-call | tf_op jit(solution)/shard_map/pallas_call | solution.py:565
  53.1 1.5 %copy.16 = bf16[8,4096]{1,0:T(8,128)(2,1)} copy(bf16[8,4096]{1,0:T(8,128)(2,1)} %get-tuple-element.4) | data formatting | bytes 131072
  54.6 1.4 %copy.17 = bf16[32,512]{1,0:T(8,128)(2,1)} copy(bf16[32,512]{1,0:T(8,128)(2,1)} %get-tuple-element.5) | data formatting | bytes 65536

commit v4 on v3

--- a/solution.py
+++ b/solution.py
@@ -375,6 +375,7 @@
 
     span = width // CHUNKS
     piece = span // 2
+    paired = groups // 2
     r1, r2, r3, s_copies = {}, {}, {}, {}
 
     def expert_chunk(t):
@@ -395,29 +396,37 @@
         r1[t].wait_recv()
         total = part[t, core].astype(jnp.float32) + got_core[t].astype(jnp.float32)
         sum_core[t] = total.astype(jnp.bfloat16)
-        first_chip, first_dev = (x_chip, x_dev) if t % 2 == 0 else (y_chip, y_dev)
-        for kind, chip_to in ((1, d_chip), (0, first_chip)):
-            r2[t, kind] = send(
-                sum_core.at[t, chip_to],
-                got_chip.at[t, kind],
-                r2_send.at[t, kind],
-                r2_recv.at[t, kind],
-                first_dev,
+        for kind, chips_to in ((1, (d_chip, d_chip)), (0, (x_chip, y_chip))):
+            for side in range(2):
+                some = pl.ds(side * paired, paired)
+                r2[t, kind, side] = send(
+                    sum_core.at[t, chips_to[side], some],
+                    got_chip.at[t, kind, some],
+                    r2_send.at[t, kind, side],
+                    r2_recv.at[t, kind, side],
+                    (x_dev, y_dev)[side],
+                )
+
+    def mid_chunk(t):
+        for side in range(2):
+            some = pl.ds(side * paired, paired)
+            r2[t, 1, side].wait_recv()
+            total = sum_core[t, (y_chip, x_chip)[side], some].astype(jnp.float32)
+            total = total + got_chip[t, 1, some].astype(jnp.float32)
+            sum_mid[t, some] = total.astype(jnp.bfloat16)
+            r2[t, 2, side] = send(
+                sum_mid.at[t, some],
+                got_chip.at[t, 2, some],
+                r2_send.at[t, 2, side],
+                r2_recv.at[t, 2, side],
+                (y_dev, x_dev)[side],
             )
-
-    def mid_chunk(t):
-        second_chip, second_dev = (y_chip, y_dev) if t % 2 == 0 else (x_chip, x_dev)
-        r2[t, 1].wait_recv()
-        total = sum_core[t, second_chip].astype(jnp.float32) + got_chip[t, 1].astype(jnp.float32)
-        sum_mid[t] = total.astype(jnp.bfloat16)
-        r2[t, 2] = send(
-            sum_mid.at[t], got_chip.at[t, 2], r2_send.at[t, 2], r2_recv.at[t, 2], second_dev
-        )
 
     def z_chunk(t):
         total = sum_core[t, chip].astype(jnp.float32)
         for kind in (0, 2):
-            r2[t, kind].wait_recv()
+            for side in range(2):
+                r2[t, kind, side].wait_recv()
             total = total + got_chip[t, kind].astype(jnp.float32)
         sum_chip[t] = total.astype(jnp.bfloat16)
         for k in range(1, groups):
@@ -606,8 +615,8 @@
             dma((4, groups)),
             dma((CHUNKS,)),
             dma((CHUNKS,)),
-            dma((CHUNKS, 3)),
-            dma((CHUNKS, 3)),
+            dma((CHUNKS, 3, 2)),
+            dma((CHUNKS, 3, 2)),
             dma((CHUNKS, groups)),
             dma((CHUNKS, groups)),
             dma((CHUNKS, groups)),

time: 56.2 us -> 56.1 us (level)
  no operation moved by 1% of the time
where the time goes in v4:
time: 56.1 us; the launch traced here: 55.9 us
  Pallas kernels  52.4 us (93%)
  local copies, waits for them, and re-layouts  2.85 us (5%)
  between operations  0.64 us (1%)
    pallas_call x1, Pallas kernels, fused_device(): pl.pallas_call(functools.partial(fused_kernel, groups), out_shape=(jax.Sh...  52.4 us
    unnamed x2, local copies, waits for them, and re-layouts  2.85 us

profile of v4, /device:TPU:0, one launch (start us, length us, event | category | flops | bytes accessed | tf_op | source)
XLA Modules:
  0.0 55.9 jit_solution(1097427059839280095)
XLA Ops:
  0.6 52.4 %shard_map.131 = (bf16[8,4096]{1,0:T(8,128)(2,1)}, bf16[32,512]{1,0:T(8,128)(2,1)}) custom-call(bf16[8,4096]{1,0:T(8,128)(2,1)} %tokens_hbm.1, s32[4,8]{1,0:T(4,128)} %bitcast.7, f32[4,8]{1,0:T(4,128)} %bitcast.8, s32[1,32]{1,0:T(1,128)} %bitcast.9, bf16[1,4096,384]{2,1,0:T(8,128)(2,1)} %gate_hbm.1, bf16[1,4096,384]{2,1,0:T(8,128)(2,1)} %up_hbm.1, ...), custom_call_target="tpu_custom_call" | custom-call | tf_op jit(solution)/shard_map/pallas_call | solution.py:574
  53.0 1.5 %copy.16 = bf16[8,4096]{1,0:T(8,128)(2,1)} copy(bf16[8,4096]{1,0:T(8,128)(2,1)} %get-tuple-element.4) | data formatting | bytes 131072
  54.5 1.4 %copy.17 = bf16[32,512]{1,0:T(8,128)(2,1)} copy(bf16[32,512]{1,0:T(8,128)(2,1)} %get-tuple-element.5) | data formatting | bytes 65536

commit v5 on v4

--- a/solution.py
+++ b/solution.py
@@ -326,18 +326,12 @@
         spread(k)
         forward(k - 1)
     forward(groups - 1)
-    for k in range(groups):
-        d_copies[k].wait_recv()
-        share(3, d_chip, k)
-    for k in range(groups):
-        for kind in range(4):
-            c_copies[kind, k].wait_recv()
-
     group_rows = groups * rows_n
-
-    def unpack(block, carry):
-        c, h = block // CHIPS, block % CHIPS
-        start = pl.multiple_of(block * group_rows, group_rows)
+    core_rows = CHIPS * group_rows
+    tile = 256
+
+    def unpack(c, h):
+        start = pl.multiple_of((c * CHIPS + h) * group_rows, group_rows)
         for side in range(2):
             got = rows_in[c, h, :, :, 0:half].astype(jnp.float32)
             got = got[:, side * rows_n : (side + 1) * rows_n].reshape(group_rows, half)
@@ -348,29 +342,41 @@
         weight_all[pl.ds(start, group_rows), :] = (extra[:, :rows_n] + extra[:, rows_n:]).reshape(
             group_rows, 128
         )
-        return carry
-
-    lax.fori_loop(0, CORES * CHIPS, unpack, 0)
-
+
+    def first_layer(c):
+        some = pl.ds(pl.multiple_of(c * core_rows, core_rows), core_rows)
+
+        def first(n, carry):
+            cols = pl.ds(pl.multiple_of(n * tile, tile), tile)
+            hidden[some, cols] = jnp.dot(
+                rows_all[some, :], w_in[:, cols], preferred_element_type=jnp.float32
+            )
+            return carry
+
+        lax.fori_loop(0, 2 * unit // tile, first, 0)
+        table_all = weight_all[some, :]
+        picked = lax.broadcasted_iota(jnp.int32, table_all.shape, 1) == me_e
+        row_weight = jnp.sum(jnp.where(picked, table_all, 0.0), axis=-1, keepdims=True)
+        gate_val = hidden[some, 0:unit]
+        active[some, :] = (
+            gate_val / (1.0 + jnp.exp(-gate_val)) * hidden[some, unit : 2 * unit] * row_weight
+        ).astype(jnp.bfloat16)
+
+    unpack(core, chip)
+    unpack(core, x_chip)
+    unpack(core, y_chip)
+    for k in range(groups):
+        d_copies[k].wait_recv()
+        share(3, d_chip, k)
+    unpack(core, d_chip)
     loads[4].wait()
     loads[5].wait()
-    tile = 256
-
-    def first(n, carry):
-        cols = pl.ds(pl.multiple_of(n * tile, tile), tile)
-        hidden[:, cols] = jnp.dot(
-            rows_all[...], w_in[:, cols], preferred_element_type=jnp.float32
-        )
-        return carry
-
-    lax.fori_loop(0, 2 * unit // tile, first, 0)
-    table_all = weight_all[...]
-    picked = lax.broadcasted_iota(jnp.int32, table_all.shape, 1) == me_e
-    row_weight = jnp.sum(jnp.where(picked, table_all, 0.0), axis=-1, keepdims=True)
-    gate_val = hidden[:, 0:unit]
-    active[...] = (
-        gate_val / (1.0 + jnp.exp(-gate_val)) * hidden[:, unit : 2 * unit] * row_weight
-    ).astype(jnp.bfloat16)
+    first_layer(core)
+    for kind, chip_of in enumerate((chip, x_chip, y_chip, d_chip)):
+        for k in range(groups):
+            c_copies[kind, k].wait_recv()
+        unpack(1 - core, chip_of)
+    first_layer(1 - core)
     loads[6].wait()
 
     span = width // CHUNKS
@@ -378,19 +384,26 @@
     paired = groups // 2
     r1, r2, r3, s_copies = {}, {}, {}, {}
 
-    def expert_chunk(t):
-        blocks_n = CORES * CHIPS * groups
+    def expert_half(t, c):
+        some = pl.ds(pl.multiple_of(c * core_rows, core_rows), core_rows)
+        outs = []
         for side in range(2):
             lower = t * span + side * piece
-            out = jnp.dot(
-                active[...], w_out[:, lower : lower + piece], preferred_element_type=jnp.float32
-            ).reshape(CORES, CHIPS, groups, rows_n, piece)
-            if side == 0:
-                top = out
-        part[t] = jnp.concatenate([top, out], axis=3).astype(jnp.bfloat16)
+            outs.append(
+                jnp.dot(
+                    active[some, :],
+                    w_out[:, lower : lower + piece],
+                    preferred_element_type=jnp.float32,
+                ).reshape(CHIPS, groups, rows_n, piece)
+            )
+        part[t, c] = jnp.concatenate(outs, axis=2).astype(jnp.bfloat16)
+
+    def expert_chunk(t):
+        expert_half(t, 1 - core)
         r1[t] = send(
             part.at[t, 1 - core], got_core.at[t], r1_send.at[t], r1_recv.at[t], sibling
         )
+        expert_half(t, core)
 
     def chip_chunk(t):
         r1[t].wait_recv()

time: 56.1 us -> 55.1 us (0.982)
  Pallas kernels: 52.4 us -> 51.4 us
    pallas_call x1, Pallas kernels: 52.4 us -> 51.4 us  [fused_device(): pl.pallas_call(functools.partial(fused_kernel, groups), out_shape=(jax.Sh...]
where the time goes in v5:
time: 55.1 us; the launch traced here: 54.9 us
  Pallas kernels  51.4 us (93%)
  local copies, waits for them, and re-layouts  2.85 us (5%)
  between operations  0.64 us (1%)
    pallas_call x1, Pallas kernels, fused_device(): pl.pallas_call(functools.partial(fused_kernel, groups), out_shape=(jax.Sh...  51.4 us
    unnamed x2, local copies, waits for them, and re-layouts  2.85 us

profile of v5, /device:TPU:0, one launch (start us, length us, event | category | flops | bytes accessed | tf_op | source)
XLA Modules:
  0.0 54.9 jit_solution(1473166554677383254)
XLA Ops:
  0.6 51.4 %shard_map.131 = (bf16[8,4096]{1,0:T(8,128)(2,1)}, bf16[32,512]{1,0:T(8,128)(2,1)}) custom-call(bf16[8,4096]{1,0:T(8,128)(2,1)} %tokens_hbm.1, s32[4,8]{1,0:T(4,128)} %bitcast.7, f32[4,8]{1,0:T(4,128)} %bitcast.8, s32[1,32]{1,0:T(1,128)} %bitcast.9, bf16[1,4096,384]{2,1,0:T(8,128)(2,1)} %gate_hbm.1, bf16[1,4096,384]{2,1,0:T(8,128)(2,1)} %up_hbm.1, ...), custom_call_target="tpu_custom_call" | custom-call | tf_op jit(solution)/shard_map/pallas_call | solution.py:587
  52.1 1.5 %copy.16 = bf16[8,4096]{1,0:T(8,128)(2,1)} copy(bf16[8,4096]{1,0:T(8,128)(2,1)} %get-tuple-element.4) | data formatting | bytes 131072
  53.5 1.4 %copy.17 = bf16[32,512]{1,0:T(8,128)(2,1)} copy(bf16[32,512]{1,0:T(8,128)(2,1)} %get-tuple-element.5) | data formatting | bytes 65536

commit v6 on v5

--- a/solution.py
+++ b/solution.py
@@ -145,7 +145,7 @@
 
 CORES = 2
 CHIPS = 4
-CHUNKS = 4
+CHUNKS = 2
 MESH = pl.DeviceIdType.MESH
 
 

time: 55.1 us -> 56.3 us (1.022)
  Pallas kernels: 51.4 us -> 52.6 us
    pallas_call x1, Pallas kernels: 51.4 us -> 52.6 us  [fused_device(): pl.pallas_call(functools.partial(fused_kernel, groups), out_shape=(jax.Sh...]
where the time goes in v6:
time: 56.3 us; the launch traced here: 56 us
  Pallas kernels  52.6 us (93%)
  local copies, waits for them, and re-layouts  2.85 us (5%)
  between operations  0.64 us (1%)
    pallas_call x1, Pallas kernels, fused_device(): pl.pallas_call(functools.partial(fused_kernel, groups), out_shape=(jax.Sh...  52.6 us
    unnamed x2, local copies, waits for them, and re-layouts  2.85 us

profile of v6, /device:TPU:0, one launch (start us, length us, event | category | flops | bytes accessed | tf_op | source)
XLA Modules:
  0.0 56.0 jit_solution(11581414684505033393)
XLA Ops:
  0.6 52.6 %shard_map.131 = (bf16[8,4096]{1,0:T(8,128)(2,1)}, bf16[32,512]{1,0:T(8,128)(2,1)}) custom-call(bf16[8,4096]{1,0:T(8,128)(2,1)} %tokens_hbm.1, s32[4,8]{1,0:T(4,128)} %bitcast.7, f32[4,8]{1,0:T(4,128)} %bitcast.8, s32[1,32]{1,0:T(1,128)} %bitcast.9, bf16[1,4096,384]{2,1,0:T(8,128)(2,1)} %gate_hbm.1, bf16[1,4096,384]{2,1,0:T(8,128)(2,1)} %up_hbm.1, ...), custom_call_target="tpu_custom_call" | custom-call | tf_op jit(solution)/shard_map/pallas_call | solution.py:587
  53.2 1.5 %copy.16 = bf16[8,4096]{1,0:T(8,128)(2,1)} copy(bf16[8,4096]{1,0:T(8,128)(2,1)} %get-tuple-element.4) | data formatting | bytes 131072
  54.7 1.4 %copy.17 = bf16[32,512]{1,0:T(8,128)(2,1)} copy(bf16[32,512]{1,0:T(8,128)(2,1)} %get-tuple-element.5) | data formatting | bytes 65536

commit v7 on v5

--- a/solution.py
+++ b/solution.py
@@ -228,6 +228,7 @@
     sibling = (chip * CORES + (1 - core), g)
     x_dev = (x_chip * CORES + core, g)
     y_dev = (y_chip * CORES + core, g)
+    d_dev = (d_chip * CORES + core, g)
 
     def z_of(step):
         return (g + step) % groups
@@ -240,7 +241,7 @@
         loads.append(copy)
 
     barrier = pltpu.get_barrier_semaphore()
-    peers = [sibling, x_dev, y_dev] + [(me_e, z_of(k)) for k in range(1, groups)]
+    peers = [sibling, x_dev, y_dev, d_dev] + [(me_e, z_of(k)) for k in range(1, groups)]
     for peer in peers:
         pl.semaphore_signal(barrier, inc=1, device_id=peer, device_id_type=MESH)
 
@@ -306,15 +307,17 @@
     def spread(step):
         x_copies[step] = row_send(chip, step, x_send.at[step], x_recv.at[step], x_dev)
         y_copies[step] = row_send(chip, step, y_send.at[step], y_recv.at[step], y_dev)
+        if step == groups - 1:
+            d_copies[step] = row_send(chip, step, d_send.at[step], d_recv.at[step], d_dev)
         share(0, chip, step)
 
     def forward(step):
         x_copies[step].wait_recv()
-        if step % 2 == 1:
+        if step % 2 == 1 and step < groups - 1:
             d_copies[step] = row_send(x_chip, step, d_send.at[step], d_recv.at[step], y_dev)
         share(1, x_chip, step)
         y_copies[step].wait_recv()
-        if step % 2 == 0:
+        if step % 2 == 0 and step < groups - 1:
             d_copies[step] = row_send(y_chip, step, d_send.at[step], d_recv.at[step], x_dev)
         share(2, y_chip, step)
 

time: 55.1 us -> 55 us (level)
  no operation moved by 1% of the time
where the time goes in v7:
time: 55 us; the launch traced here: 54.8 us
  Pallas kernels  51.3 us (93%)
  local copies, waits for them, and re-layouts  2.85 us (5%)
  between operations  0.64 us (1%)
    pallas_call x1, Pallas kernels, fused_device(): pl.pallas_call(functools.partial(fused_kernel, groups), out_shape=(jax.Sh...  51.3 us
    unnamed x2, local copies, waits for them, and re-layouts  2.85 us

profile of v7, /device:TPU:0, one launch (start us, length us, event | category | flops | bytes accessed | tf_op | source)
XLA Modules:
  0.0 54.8 jit_solution(12594034374123701416)
XLA Ops:
  0.6 51.3 %shard_map.131 = (bf16[8,4096]{1,0:T(8,128)(2,1)}, bf16[32,512]{1,0:T(8,128)(2,1)}) custom-call(bf16[8,4096]{1,0:T(8,128)(2,1)} %tokens_hbm.1, s32[4,8]{1,0:T(4,128)} %bitcast.7, f32[4,8]{1,0:T(4,128)} %bitcast.8, s32[1,32]{1,0:T(1,128)} %bitcast.9, bf16[1,4096,384]{2,1,0:T(8,128)(2,1)} %gate_hbm.1, bf16[1,4096,384]{2,1,0:T(8,128)(2,1)} %up_hbm.1, ...), custom_call_target="tpu_custom_call" | custom-call | tf_op jit(solution)/shard_map/pallas_call | solution.py:590
  51.9 1.5 %copy.16 = bf16[8,4096]{1,0:T(8,128)(2,1)} copy(bf16[8,4096]{1,0:T(8,128)(2,1)} %get-tuple-element.4) | data formatting | bytes 131072
  53.4 1.4 %copy.17 = bf16[32,512]{1,0:T(8,128)(2,1)} copy(bf16[32,512]{1,0:T(8,128)(2,1)} %get-tuple-element.5) | data formatting | bytes 65536

commit v8 on v7

--- a/solution.py
+++ b/solution.py
@@ -307,17 +307,17 @@
     def spread(step):
         x_copies[step] = row_send(chip, step, x_send.at[step], x_recv.at[step], x_dev)
         y_copies[step] = row_send(chip, step, y_send.at[step], y_recv.at[step], y_dev)
-        if step == groups - 1:
+        if step >= groups - 2:
             d_copies[step] = row_send(chip, step, d_send.at[step], d_recv.at[step], d_dev)
         share(0, chip, step)
 
     def forward(step):
         x_copies[step].wait_recv()
-        if step % 2 == 1 and step < groups - 1:
+        if step % 2 == 1 and step < groups - 2:
             d_copies[step] = row_send(x_chip, step, d_send.at[step], d_recv.at[step], y_dev)
         share(1, x_chip, step)
         y_copies[step].wait_recv()
-        if step % 2 == 0 and step < groups - 1:
+        if step % 2 == 0 and step < groups - 2:
             d_copies[step] = row_send(y_chip, step, d_send.at[step], d_recv.at[step], x_dev)
         share(2, y_chip, step)
 

time: 55 us -> 55.8 us (1.015)
  Pallas kernels: 51.3 us -> 52.1 us
    pallas_call x1, Pallas kernels: 51.3 us -> 52.1 us  [fused_device(): pl.pallas_call(functools.partial(fused_kernel, groups), out_shape=(jax.Sh...]
where the time goes in v8:
time: 55.8 us; the launch traced here: 55.6 us
  Pallas kernels  52.1 us (93%)
  local copies, waits for them, and re-layouts  2.85 us (5%)
  between operations  0.64 us (1%)
    pallas_call x1, Pallas kernels, fused_device(): pl.pallas_call(functools.partial(fused_kernel, groups), out_shape=(jax.Sh...  52.1 us
    unnamed x2, local copies, waits for them, and re-layouts  2.85 us

profile of v8, /device:TPU:0, one launch (start us, length us, event | category | flops | bytes accessed | tf_op | source)
XLA Modules:
  0.0 55.6 jit_solution(2115596837525330798)
XLA Ops:
  0.6 52.1 %shard_map.131 = (bf16[8,4096]{1,0:T(8,128)(2,1)}, bf16[32,512]{1,0:T(8,128)(2,1)}) custom-call(bf16[8,4096]{1,0:T(8,128)(2,1)} %tokens_hbm.1, s32[4,8]{1,0:T(4,128)} %bitcast.7, f32[4,8]{1,0:T(4,128)} %bitcast.8, s32[1,32]{1,0:T(1,128)} %bitcast.9, bf16[1,4096,384]{2,1,0:T(8,128)(2,1)} %gate_hbm.1, bf16[1,4096,384]{2,1,0:T(8,128)(2,1)} %up_hbm.1, ...), custom_call_target="tpu_custom_call" | custom-call | tf_op jit(solution)/shard_map/pallas_call | solution.py:590
  52.7 1.5 %copy.16 = bf16[8,4096]{1,0:T(8,128)(2,1)} copy(bf16[8,4096]{1,0:T(8,128)(2,1)} %get-tuple-element.4) | data formatting | bytes 131072
  54.2 1.4 %copy.17 = bf16[32,512]{1,0:T(8,128)(2,1)} copy(bf16[32,512]{1,0:T(8,128)(2,1)} %get-tuple-element.5) | data formatting | bytes 65536
